TPU v7x, 128 devices: a whole 4x4x4 slice. The times are simulated.
128 devices in a mesh: dp: 4 (over z), mp: 32 (over x, y, core).
Axes of the slice: x: 4, y: 4, z: 4, core: 2. Of those that a mesh axis runs over, the one named last changes fastest.
Arguments:
- tokens: bfloat16 [16384, 4096], P(('dp', 'mp')), may hold values from -6 to 6
- expert_ids: int32 [16384, 1], P(('dp', 'mp')), may hold values from 0 to 63; in each aligned block of 128 rows (0 to 127, 128 to 255, ...) at most 3 rows name the same one
- gate_probs: float32 [16384, 1], P(('dp', 'mp')), may hold values from 0.3 to 1
- gate_weight: bfloat16 [64, 4096, 1536], P('mp', None, 'dp'), may hold values from -0.09375 to 0.09375
- up_weight: bfloat16 [64, 4096, 1536], P('mp', None, 'dp'), may hold values from -0.09375 to 0.09375
- down_weight: bfloat16 [64, 1536, 4096], P('mp', 'dp'), may hold values from -0.15625 to 0.15625
- sign_offset: int32 [1], replicated, may hold values from 1 to 999999999
Outputs:
- out_plus: bfloat16 [16384, 4096], P(('dp', 'mp'))
- out_minus: bfloat16 [16384, 4096], P(('dp', 'mp'))
Inputs may be any that keep to these rules, and one draw needn't show every extreme that they name: `expert_ids`: within each aligned block of 128 tokens (the tokens of one device) no expert is named by more than 3 routes, a bound that some block reaches.
All inputs are finite; a program needn't handle non-finite values.
Results may differ from a plain program's by a relative error of at most 0.01.
Values may be sent and summed in bfloat16 or wider, within the bound.
A program may use at most 128 MiB of HBM per device.

v0:
```python
import jax
import jax.numpy as jnp
from jax import lax
from jax.sharding import PartitionSpec as P

FF = 1536
epsilon_step = 0.005


def mixing(number):
    number = number ^ lax.shift_right_logical(number, jnp.full_like(number, 16))
    number = number * 73244475
    number = number ^ lax.shift_right_logical(number, jnp.full_like(number, 16))
    number = number * 73244475
    return number ^ lax.shift_right_logical(number, jnp.full_like(number, 16))


def sign_noise(offset_mixed, position, matrix_tag):
    hashed = mixing(position * 3 + matrix_tag ^ offset_mixed)
    parity = lax.shift_right_logical(hashed, jnp.full_like(hashed, 9)) & 1
    return (parity * 2 - 1).astype(jnp.float32)


def perturb(weight, noise, direction):
    return (weight.astype(jnp.float32) + direction * epsilon_step * noise).astype(jnp.bfloat16)


def expert_rows(arrived, weight_sets):
    lead_shape = arrived.shape
    model_width = lead_shape[-1]
    per_expert = []
    for local_expert in range(lead_shape[2]):
        flat_rows = arrived[:, :, local_expert].reshape(-1, model_width)
        by_pass = []
        for gate_moved, up_moved, down_moved in weight_sets[local_expert]:
            gate_act = jnp.dot(flat_rows, gate_moved, preferred_element_type=jnp.float32)
            up_act = jnp.dot(flat_rows, up_moved, preferred_element_type=jnp.float32)
            hidden = (jax.nn.silu(gate_act) * up_act).astype(jnp.bfloat16)
            by_pass.append(
                jnp.dot(hidden, down_moved, preferred_element_type=jnp.float32).astype(jnp.bfloat16)
            )
        stacked = jnp.stack(by_pass, axis=1).reshape(
            lead_shape[0], lead_shape[1], lead_shape[3], len(by_pass), model_width
        )
        per_expert.append(stacked)
    return jnp.stack(per_expert, axis=2)


def shards(tokens, expert_ids, gate_probs, gate_weight, up_weight, down_weight, sign_offset):
    mp_count = lax.axis_size("mp")
    tok_rows, model_width = tokens.shape
    route_count = expert_ids.shape[1]
    local_count = gate_weight.shape[0]
    quarter = gate_weight.shape[2]
    expert_count = local_count * mp_count
    capacity = 3 * tok_rows * route_count // (2 * expert_count)
    offset_mixed = mixing(sign_offset[0] * 668265261 + 12345)
    expert_base = lax.axis_index("mp") * local_count
    hidden_base = lax.axis_index("dp") * quarter
    width_axis = lax.broadcasted_iota(jnp.int32, (model_width, quarter), 0)
    unit_axis = lax.broadcasted_iota(jnp.int32, (model_width, quarter), 1) + hidden_base
    plus_sets = []
    minus_sets = []
    for local_expert in range(local_count):
        expert_global = expert_base + local_expert
        gate_pos = (expert_global * model_width + width_axis) * FF + unit_axis
        down_pos = (expert_global * FF + unit_axis.T) * model_width + width_axis.T
        noise_gate = sign_noise(offset_mixed, gate_pos, 0)
        noise_up = sign_noise(offset_mixed, gate_pos, 1)
        noise_down = sign_noise(offset_mixed, down_pos, 2)
        for direction, target in ((1.0, plus_sets), (-1.0, minus_sets)):
            target.append(
                (
                    perturb(gate_weight[local_expert], noise_gate, direction),
                    perturb(up_weight[local_expert], noise_up, direction),
                    perturb(down_weight[local_expert], noise_down, direction),
                )
            )
    route_flat = expert_ids.reshape(-1)
    expert_axis = lax.broadcasted_iota(jnp.int32, (route_flat.shape[0], expert_count), 1)
    onehot = (route_flat[:, None] == expert_axis).astype(jnp.int32)
    earlier = jnp.cumsum(onehot, axis=0, dtype=jnp.int32) - onehot
    rank_in = jnp.sum(earlier * onehot, axis=1, dtype=jnp.int32)
    slot_of = (route_flat * capacity + rank_in).reshape(tok_rows, route_count)
    slot_axis = lax.broadcasted_iota(jnp.int32, (expert_count * capacity, tok_rows), 0)
    selector = (slot_axis == slot_of[:, 0][None, :]).astype(jnp.float32)
    outgoing = jnp.dot(
        selector.astype(jnp.bfloat16), tokens, preferred_element_type=jnp.float32
    ).astype(jnp.bfloat16)
    outgoing = outgoing.reshape(mp_count, local_count, capacity, model_width)
    grouped = lax.all_gather(outgoing[None], "dp", axis=0, tiled=True)
    arrived = lax.all_to_all(grouped, "mp", split_axis=1, concat_axis=1, tiled=True)

    def finish(weight_sets):
        partials = expert_rows(arrived, weight_sets)
        returned = lax.all_to_all(partials, "mp", split_axis=1, concat_axis=1, tiled=True)
        summed = lax.psum_scatter(
            returned.astype(jnp.float32).astype(jnp.bfloat16), "dp", scatter_dimension=0, tiled=True
        ).astype(jnp.float32)
        return summed[0].astype(jnp.bfloat16)

    def combine(result, pass_index):
        flat_out = result.reshape(expert_count * capacity, result.shape[3], model_width)[
            :, pass_index
        ]
        picked = (
            jnp.take(flat_out, slot_of.reshape(-1), axis=0)
            .reshape(tok_rows, route_count, model_width)
            .astype(jnp.float32)
        )
        return jnp.sum(gate_probs[:, :, None] * picked, axis=1).astype(jnp.bfloat16)

    plus_result = finish([[entry_set] for entry_set in plus_sets])
    minus_result = finish([[entry_set] for entry_set in minus_sets])
    return (combine(plus_result, 0), combine(minus_result, 0))


def solution(mesh):
    in_specs = (
        P(("dp", "mp"), None),
        P(("dp", "mp"), None),
        P(("dp", "mp"), None),
        P("mp", None, "dp"),
        P("mp", None, "dp"),
        P("mp", "dp", None),
        P(),
    )
    out_specs = (P(("dp", "mp"), None), P(("dp", "mp"), None))
    return jax.shard_map(shards, mesh=mesh, in_specs=in_specs, out_specs=out_specs, check_vma=False)
```

profile of v0, /device:TPU:1, one launch (start us, length us, event | category | flops | bytes accessed | tf_op | source)
XLA Modules:
  0.0 660.6 jit_solution(3425733113894375996)
XLA Ops:
  7.2 0.8 fusion.194
  8.0 0.2 reduce_window_sum.11
  8.2 0.8 select_reduce_fusion
  9.1 1.2 compare_and_fusion
  10.2 0.5 copy-done.4
  10.8 1.7 convolution_convert_fusion.4
  12.5 2.7 broadcast_in_dim_reshape.3
  15.2 2.3 copy.13
  17.6 69.3 %all-gather.2.cloned.1.call-done = bf16[4,32,2,3,4096]{4,1,3,2,0:T(8,128)(2,1)} async-done(((bf16[1,32,2,3,4096]{4,1,3,2,0:T(8,128)(2,1)}), bf16[4,32,2,3,4096]{4,1,3,2,0:T(8,128)(2,1)}) %all-gather.2.cloned.1.call-update) | async-done | bytes 6291472 | tf_op jit(solution)/shard_map/all_gather | solution.py:91
  86.8 10.3 %copy.14 = bf16[4,32,2,3,4096]{4,0,3,2,1:T(4,128)(2,1)} copy(bf16[4,32,2,3,4096]{4,1,3,2,0:T(8,128)(2,1)} %all-gather.2.cloned.1.call-done) | data formatting | bytes 12582912 | tf_op jit(solution)/shard_map/all_gather | solution.py:91
  97.1 7.6 %all-to-all-start = ((bf16[4,32,2,3,4096]{4,0,3,2,1:T(4,128)(2,1)}), bf16[4,32,2,3,4096]{4,0,3,2,1:T(4,128)(2,1)}, u32[]{:S(2)}, u32[]{:S(2)}) async-start(bf16[4,32,2,3,4096]{4,0,3,2,1:T(4,128)(2,1)} %copy.14), calls=%async_computation | async-start | bytes 12582912 | tf_op jit(solution)/shard_map/all_to_all | solution.py:92
  104.7 0.2 reduce-scatter.3.cloned.1.call-start
  105.7 77.0 %all-to-all-done = bf16[4,32,2,3,4096]{4,0,3,2,1:T(4,128)(2,1)} async-done(((bf16[4,32,2,3,4096]{4,0,3,2,1:T(4,128)(2,1)}), bf16[4,32,2,3,4096]{4,0,3,2,1:T(4,128)(2,1)}, u32[]{:S(2)}, u32[]{:S(2)}) %all-to-all-start) | async-done | bytes 6291488 | tf_op jit(solution)/shard_map/all_to_all | solution.py:92
  182.7 6.9 %fusion.296 = (bf16[4,32,1,3,4096]{4,0,3,2,1:T(4,128)(2,1)}, bf16[4,32,1,3,4096]{4,0,3,2,1:T(4,128)(2,1)S(1)}) fusion(bf16[4,32,2,3,4096]{4,0,3,2,1:T(4,128)(2,1)} %all-to-all-done), kind=kLoop, calls=%fused_computation.284 | loop fusion | bytes 12582912 | tf_op jit(solution)/shard_map/slice | solution.py:33
  189.6 4.6 copy.16
  194.3 7.4 %reshape_squeeze.9 = bf16[384,4096]{1,0:T(8,128)(2,1)} reshape(bf16[4,32,1,3,4096]{4,3,1,0,2:T(4,128)(2,1)} %copy.16) | data formatting | bytes 6291456 | tf_op jit(solution)/shard_map/reshape;squeeze | solution.py:33
  201.7 7.5 %fusion.118 = f32[384,384]{1,0:T(8,128)S(1)} fusion(bf16[384,4096]{1,0:T(8,128)(2,1)} %reshape_squeeze.9, s32[4096]{0:T(1024)S(1)} %add_multiply_fusion.2, s32[]{:T(128)S(6)} %xor.269, s32[384]{0:T(512)S(1)} %iota_add_fusion, bf16[2,4096,384]{2,1,0:T(8,128)(2,1)} %param.12), kind=kOutput, calls=%fused_computation.151 | convolution fusion | flops 1239416832 | bytes 6899204 | tf_op jit(solution)/shard_map/dot_general | solution.py:36
  209.2 15.7 %convolution_convert_fusion.2 = bf16[384,4096]{1,0:T(8,128)(2,1)} fusion(s32[384]{0:T(512)S(1)} %get-tuple-element.9, s32[]{:T(128)S(6)} %xor.269, bf16[2,384,4096]{2,1,0:T(8,128)(2,1)} %param.14, bf16[384,4096]{1,0:T(8,128)(2,1)} %reshape_squeeze.9, s32[4096]{0:T(1024)S(1)} %add_multiply_fusion.2, s32[384]{0:T(512)S(1)} %iota_add_fusion, ...), kind=kOutput, calls=%fused_computation.92 | convolution fusion | flops 2484436992 | bytes 13193216 | tf_op jit(solution)/shard_map/dot_general | solution.py:40
  224.9 7.1 %stack_reshape_stack.13 = bf16[4,32,1,3,1,4096]{5,3,1,0,4,2:T(4,128)(2,1)} reshape(bf16[384,4096]{1,0:T(8,128)(2,1)} %convolution_convert_fusion.2) | data formatting | bytes 6291456 | tf_op jit(solution)/shard_map/stack;reshape;stack | solution.py:46
  232.0 7.4 %copy.15 = bf16[4,32,1,3,4096]{4,3,1,0,2:T(4,128)(2,1)} copy(bf16[4,32,1,3,4096]{4,0,3,2,1:T(4,128)(2,1)} %get-tuple-element.5) | data formatting | bytes 6291456 | tf_op jit(solution)/shard_map/slice | solution.py:33
  239.4 7.4 %reshape_squeeze.8 = bf16[384,4096]{1,0:T(8,128)(2,1)} reshape(bf16[4,32,1,3,4096]{4,3,1,0,2:T(4,128)(2,1)} %copy.15) | data formatting | bytes 6291456 | tf_op jit(solution)/shard_map/reshape;squeeze | solution.py:33
  246.8 7.5 %fusion.110 = f32[384,384]{1,0:T(8,128)S(1)} fusion(bf16[384,4096]{1,0:T(8,128)(2,1)} %reshape_squeeze.8, s32[]{:T(128)S(6)} %xor.269, s32[384]{0:T(512)S(1)} %iota_add_fusion, s32[4096]{0:T(1024)S(1)} %add_multiply_fusion.3, bf16[2,4096,384]{2,1,0:T(8,128)(2,1)} %param.12), kind=kOutput, calls=%fused_computation.147 | convolution fusion | flops 1239416832 | bytes 6899204 | tf_op jit(solution)/shard_map/dot_general | solution.py:36
  254.3 15.5 %convolution_convert_fusion.3 = bf16[384,4096]{1,0:T(8,128)(2,1)} fusion(s32[]{:T(128)S(6)} %xor.269, s32[384]{0:T(512)S(1)} %get-tuple-element.10, bf16[2,384,4096]{2,1,0:T(8,128)(2,1)} %param.14, bf16[384,4096]{1,0:T(8,128)(2,1)} %reshape_squeeze.8, s32[384]{0:T(512)S(1)} %iota_add_fusion, s32[4096]{0:T(1024)S(1)} %add_multiply_fusion.3, ...), kind=kOutput, calls=%fused_computation.93 | convolution fusion | flops 2484436992 | bytes 13193216 | tf_op jit(solution)/shard_map/dot_general | solution.py:40
  269.8 7.1 %stack_reshape_stack.12 = bf16[4,32,1,3,1,4096]{5,3,1,0,4,2:T(4,128)(2,1)} reshape(bf16[384,4096]{1,0:T(8,128)(2,1)} %convolution_convert_fusion.3) | data formatting | bytes 6291456 | tf_op jit(solution)/shard_map/stack;reshape;stack | solution.py:46
  276.9 8.7 %pad_maximum_fusion = bf16[4,32,2,3,1,4096]{5,3,1,0,4,2:T(4,128)(2,1)} fusion(bf16[4,32,1,3,1,4096]{5,3,1,0,4,2:T(4,128)(2,1)} %stack_reshape_stack.13, bf16[4,32,1,3,1,4096]{5,3,1,0,4,2:T(4,128)(2,1)} %stack_reshape_stack.12), kind=kLoop, calls=%fused_computation.20 | loop fusion | flops 3145728 | bytes 12582912 | tf_op jit(solution)/shard_map/stack | solution.py:46
  285.6 21.7 %copy.17 = bf16[4,32,2,3,1,4096]{5,0,4,3,2,1:T(4,128)(2,1)} copy(bf16[4,32,2,3,1,4096]{5,3,1,0,4,2:T(4,128)(2,1)} %pad_maximum_fusion) | data formatting | bytes 12582912 | tf_op jit(solution)/shard_map/stack | solution.py:46
  307.3 87.6 %all_to_all.15 = bf16[4,32,2,3,1,4096]{5,0,4,3,2,1:T(4,128)(2,1)S(1)} all-to-all(bf16[4,32,2,3,1,4096]{5,0,4,3,2,1:T(4,128)(2,1)} %copy.17), channel_id=1, replica_groups=mesh['dp'=4,'mp'=32] {'mp'}, dimensions={1} | all-to-all | bytes 12582912 | tf_op jit(solution)/shard_map/all_to_all | solution.py:96
  394.9 6.1 copy.18
  401.1 0.0 reduce-scatter.5.cloned.1.call-start
  401.2 7.5 %fusion.120 = f32[384,384]{1,0:T(8,128)S(1)} fusion(bf16[384,4096]{1,0:T(8,128)(2,1)} %reshape_squeeze.9, s32[4096]{0:T(1024)S(1)} %add_multiply_fusion.2, s32[]{:T(128)S(6)} %xor.269, s32[384]{0:T(512)S(1)} %iota_add_fusion, bf16[2,4096,384]{2,1,0:T(8,128)(2,1)} %param.12), kind=kOutput, calls=%fused_computation.152 | convolution fusion | flops 1239416832 | bytes 6899204 | tf_op jit(solution)/shard_map/dot_general | solution.py:36
  408.7 15.5 %convolution_convert_fusion = bf16[384,4096]{1,0:T(8,128)(2,1)} fusion(s32[384]{0:T(512)S(1)} %get-tuple-element.9, s32[]{:T(128)S(6)} %xor.269, bf16[2,384,4096]{2,1,0:T(8,128)(2,1)} %param.14, bf16[384,4096]{1,0:T(8,128)(2,1)} %reshape_squeeze.9, s32[4096]{0:T(1024)S(1)} %add_multiply_fusion.2, s32[384]{0:T(512)S(1)} %iota_add_fusion, ...), kind=kOutput, calls=%fused_computation.90 | convolution fusion | flops 2484436992 | bytes 13193216 | tf_op jit(solution)/shard_map/dot_general | solution.py:40
  424.2 7.1 %stack_reshape_stack.15 = bf16[4,32,1,3,1,4096]{5,3,1,0,4,2:T(4,128)(2,1)} reshape(bf16[384,4096]{1,0:T(8,128)(2,1)} %convolution_convert_fusion) | data formatting | bytes 6291456 | tf_op jit(solution)/shard_map/stack;reshape;stack | solution.py:46
  431.3 7.6 %fusion.112 = f32[384,384]{1,0:T(8,128)S(1)} fusion(bf16[384,4096]{1,0:T(8,128)(2,1)} %reshape_squeeze.8, s32[]{:T(128)S(6)} %xor.269, s32[384]{0:T(512)S(1)} %iota_add_fusion, s32[4096]{0:T(1024)S(1)} %add_multiply_fusion.3, bf16[2,4096,384]{2,1,0:T(8,128)(2,1)} %param.12), kind=kOutput, calls=%fused_computation.148 | convolution fusion | flops 1239416832 | bytes 6899204 | tf_op jit(solution)/shard_map/dot_general | solution.py:36
  438.9 15.9 %convolution_convert_fusion.1 = bf16[384,4096]{1,0:T(8,128)(2,1)} fusion(s32[]{:T(128)S(6)} %xor.269, s32[384]{0:T(512)S(1)} %get-tuple-element.10, bf16[2,384,4096]{2,1,0:T(8,128)(2,1)} %param.14, bf16[384,4096]{1,0:T(8,128)(2,1)} %reshape_squeeze.8, s32[384]{0:T(512)S(1)} %iota_add_fusion, s32[4096]{0:T(1024)S(1)} %add_multiply_fusion.3, ...), kind=kOutput, calls=%fused_computation.91 | convolution fusion | flops 2484436992 | bytes 13193216 | tf_op jit(solution)/shard_map/dot_general | solution.py:40
  454.8 7.1 %stack_reshape_stack.14 = bf16[4,32,1,3,1,4096]{5,3,1,0,4,2:T(4,128)(2,1)} reshape(bf16[384,4096]{1,0:T(8,128)(2,1)} %convolution_convert_fusion.1) | data formatting | bytes 6291456 | tf_op jit(solution)/shard_map/stack;reshape;stack | solution.py:46
  461.9 8.8 %pad_maximum_fusion.1 = bf16[4,32,2,3,1,4096]{5,3,1,0,4,2:T(4,128)(2,1)} fusion(bf16[4,32,1,3,1,4096]{5,3,1,0,4,2:T(4,128)(2,1)} %stack_reshape_stack.15, bf16[4,32,1,3,1,4096]{5,3,1,0,4,2:T(4,128)(2,1)} %stack_reshape_stack.14), kind=kLoop, calls=%fused_computation.21 | loop fusion | flops 3145728 | bytes 12582912 | tf_op jit(solution)/shard_map/stack | solution.py:46
  470.6 21.3 %copy.20 = bf16[4,32,2,3,1,4096]{5,0,4,3,2,1:T(4,128)(2,1)} copy(bf16[4,32,2,3,1,4096]{5,3,1,0,4,2:T(4,128)(2,1)} %pad_maximum_fusion.1) | data formatting | bytes 12582912 | tf_op jit(solution)/shard_map/stack | solution.py:46
  492.0 78.0 %all_to_all.16 = bf16[4,32,2,3,1,4096]{5,0,4,3,2,1:T(4,128)(2,1)S(1)} all-to-all(bf16[4,32,2,3,1,4096]{5,0,4,3,2,1:T(4,128)(2,1)} %copy.20), channel_id=1, replica_groups=mesh['dp'=4,'mp'=32] {'mp'}, dimensions={1} | all-to-all | bytes 12582912 | tf_op jit(solution)/shard_map/all_to_all | solution.py:96
  569.9 6.1 copy.21
  576.1 0.6 copy-done.5
  576.7 4.1 copy.19
  580.8 3.3 convert_element_type.262
  584.1 53.3 %reduce-scatter.5.cloned.1.call-done = bf16[1,32,2,3,1,4096]{5,1,4,3,2,0:T(8,128)(2,1)} async-done(((bf16[4,32,2,3,1,4096]{5,1,4,3,2,0:T(8,128)(2,1)}), bf16[1,32,2,3,1,4096]{5,1,4,3,2,0:T(8,128)(2,1)}) %reduce-scatter.5.cloned.1.call-update) | async-done | bytes 1572880 | tf_op jit(solution)/shard_map/reduce_scatter | solution.py:97
  637.4 4.1 copy.22
  641.5 4.3 convert_element_type.279
  645.8 2.2 gather_fusion
  648.0 3.9 gather_fusion.1
  651.9 1.9 multiply_convert_fusion
  (23 shorter events, 0.2 us)
Async XLA Ops:
  7.2 3.6 copy-start
  7.2 79.6 %all-gather.2.cloned.1.call-start = ((), (), s32[]{:S(2)}) async-start(), calls=%async_computation.5 | async-start | bytes 7864320 | tf_op jit(solution)/shard_map/all_gather | solution.py:91
  10.2 0.5 copy-start.4
  97.1 85.6 %all-to-all-start = ((bf16[4,32,2,3,4096]{4,0,3,2,1:T(4,128)(2,1)}), bf16[4,32,2,3,4096]{4,0,3,2,1:T(4,128)(2,1)}, u32[]{:S(2)}, u32[]{:S(2)}) async-start(bf16[4,32,2,3,4096]{4,0,3,2,1:T(4,128)(2,1)} %copy.14), calls=%async_computation | async-start | bytes 12582912 | tf_op jit(solution)/shard_map/all_to_all | solution.py:92
  104.7 471.9 %reduce-scatter.3.cloned.1.call-start = ((), (), s32[]{:S(2)}) async-start(), calls=%async_computation.6 | async-start | bytes 7864320 | tf_op jit(solution)/shard_map/reduce_scatter | solution.py:97
  401.1 236.3 %reduce-scatter.5.cloned.1.call-start = ((), (), s32[]{:S(2)}) async-start(), calls=%async_computation.7 | async-start | bytes 7864320 | tf_op jit(solution)/shard_map/reduce_scatter | solution.py:97
  576.0 0.6 copy-start.5
  645.8 8.0 %copy-start.1 = (bf16[128,4096]{1,0:T(8,128)(2,1)S(1)}, bf16[128,4096]{1,0:T(8,128)(2,1)}, u32[]{:S(2)}) copy-start(bf16[128,4096]{1,0:T(8,128)(2,1)} %param.9) | copy-start | bytes 3145732
  648.0 3.9 copy-start.2
  648.0 3.9 copy-start.3
  648.0 3.9 copy-start.6
Sparse Core Ops, SparseCore 0:
  17.7 69.0 all-gather.1
  401.2 61.1 reduce-scatter.2
  576.2 61.2 reduce-scatter.4
where the time goes:
time: 668 us; the launch traced here: 661 us
  waiting for transfers between devices  200 us (30%)
  blocking collectives  166 us (25%)
  local copies, waits for them, and re-layouts  156 us (23%)
  matrix products  94.5 us (14%)
  other arithmetic  22.4 us (3%)
  between operations  14.8 us (2%)
  starting transfers between devices  7.92 us (1%)
    all_to_all x2, blocking collectives, finish(): lax.all_to_all(partials, 'mp', split_axis=1, concat_axis=1, tiled=True)  166 us
    all_to_all x1, waiting for transfers between devices, shards(): lax.all_to_all(grouped, 'mp', split_axis=1, concat_axis=1, tiled=True)  77 us
    another operation x6, local copies, waits for them, and re-layouts, expert_rows(): return jnp.stack(per_expert, axis=2)  71.4 us
    all_gather x1, waiting for transfers between devices, shards(): grouped = lax.all_gather(outgoing[None], 'dp', axis=0, tiled=True)  69.3 us
    dot_general x4, matrix products, expert_rows(): jnp.dot(hidden, down_moved, preferred_element_type=jnp.float32)  62.6 us
    reduce_scatter x2, waiting for transfers between devices, finish(): lax.psum_scatter(returned.astype(jnp.float32).astype(jnp.bfloat16), 'dp',...  53.4 us
    dot_general x4, matrix products, expert_rows(): jnp.dot(flat_rows, gate_moved, preferred_element_type=jnp.float32)  30.1 us
    slice x3, local copies, waits for them, and re-layouts, expert_rows(): flat_rows = arrived[:, :, local_expert].reshape(-1, model_width)  19 us
  transfers between devices with their start and end apart: 4, of which 3 were waited for; matrix products, arithmetic and copies ran while one was open for 16% of the time, Pallas kernels for 0%

commit v1 on v0

--- a/solution.py
+++ b/solution.py
@@ -2,6 +2,7 @@
 import jax.numpy as jnp
 from jax import lax
 from jax.sharding import PartitionSpec as P
+from jax.lax import all_to_all, axis_size
 
 FF = 1536
 epsilon_step = 0.005
@@ -88,7 +89,10 @@
         selector.astype(jnp.bfloat16), tokens, preferred_element_type=jnp.float32
     ).astype(jnp.bfloat16)
     outgoing = outgoing.reshape(mp_count, local_count, capacity, model_width)
-    grouped = lax.all_gather(outgoing[None], "dp", axis=0, tiled=True)
+    arr_in = outgoing[None]
+    f_next = axis_size("dp")
+    outer = all_to_all(jnp.stack([arr_in] * f_next, axis=0), "dp", 0, 0)
+    grouped = jnp.concatenate(outer, axis=0)
     arrived = lax.all_to_all(grouped, "mp", split_axis=1, concat_axis=1, tiled=True)
 
     def finish(weight_sets):

time: 668 us -> 676 us (1.012)
  blocking collectives: 166 us -> 241 us
  waiting for transfers between devices: 200 us -> 130 us
    all_to_all x0 -> x1, blocking collectives: none -> 76.1 us  [shards(): outer = all_to_all(jnp.stack([arr_in] * f_next, axis=0), 'dp', 0, 0)]
    all_gather x1 -> x0, waiting for transfers between devices: 69.3 us -> none  [shards(): grouped = lax.all_gather(outgoing[None], 'dp', axis=0, tiled=True)]
    all_gather x1 -> x0, local copies, waits for them, and re-layouts: 10.3 us -> none  [shards(): grouped = lax.all_gather(outgoing[None], 'dp', axis=0, tiled=True)]
    reshape x0 -> x1, local copies, waits for them, and re-layouts: none -> 10.3 us  [shards(): grouped = jnp.concatenate(outer, axis=0)]
  transfers between devices with their start and end apart: 4 -> 3, of which waited for: 3 -> 2; matrix products, arithmetic and copies ran while one was open for 16% -> 16% of each run, Pallas kernels for 0% -> 0%
where the time goes in v1:
time: 676 us; the launch traced here: 667 us
  blocking collectives  241 us (36%)
  local copies, waits for them, and re-layouts  155 us (23%)
  waiting for transfers between devices  130 us (19%)
  matrix products  94.4 us (14%)
  other arithmetic  22.4 us (3%)
  between operations  15.1 us (2%)
  starting transfers between devices  9.26 us (1%)
    all_to_all x2, blocking collectives, finish(): lax.all_to_all(partials, 'mp', split_axis=1, concat_axis=1, tiled=True)  165 us
    all_to_all x1, waiting for transfers between devices, shards(): lax.all_to_all(grouped, 'mp', split_axis=1, concat_axis=1, tiled=True)  77 us
    all_to_all x1, blocking collectives, shards(): outer = all_to_all(jnp.stack([arr_in] * f_next, axis=0), 'dp', 0, 0)  76.1 us
    another operation x6, local copies, waits for them, and re-layouts, expert_rows(): return jnp.stack(per_expert, axis=2)  71.3 us
    dot_general x4, matrix products, expert_rows(): jnp.dot(hidden, down_moved, preferred_element_type=jnp.float32)  62.7 us
    reduce_scatter x2, waiting for transfers between devices, finish(): lax.psum_scatter(returned.astype(jnp.float32).astype(jnp.bfloat16), 'dp',...  52.5 us
    dot_general x4, matrix products, expert_rows(): jnp.dot(flat_rows, gate_moved, preferred_element_type=jnp.float32)  30 us
    slice x3, local copies, waits for them, and re-layouts, expert_rows(): flat_rows = arrived[:, :, local_expert].reshape(-1, model_width)  18.9 us
  transfers between devices with their start and end apart: 3, of which 2 were waited for; matrix products, arithmetic and copies ran while one was open for 16% of the time, Pallas kernels for 0%

profile of v1, /device:TPU:1, one launch (start us, length us, event | category | flops | bytes accessed | tf_op | source)
XLA Modules:
  0.0 667.5 jit_solution(7669273173260167474)
XLA Ops:
  7.2 0.8 fusion.194
  8.0 0.2 reduce_window_sum.11
  8.2 0.8 select_reduce_fusion
  9.0 1.2 compare_and_fusion
  10.2 0.6 copy-done.4
  10.8 1.7 convolution_convert_fusion.4
  12.5 2.7 stack_broadcast_in_dim_reshape.2
  15.2 1.1 copy.14
  16.4 0.8 stack.9
  17.2 76.1 %all_to_all.20 = bf16[4,1,32,2,3,4096]{5,2,4,3,1,0:T(8,128)(2,1)} all-to-all(bf16[4,1,32,2,3,4096]{5,2,4,3,1,0:T(8,128)(2,1)S(1)} %stack.9), channel_id=1, replica_groups=mesh['dp'=4,'mp'=32] {'dp'}, dimensions={0} | all-to-all | bytes 12582912 | tf_op jit(solution)/shard_map/all_to_all | solution.py:94
  93.3 10.3 %copy.15 = bf16[4,32,2,3,4096]{4,0,3,2,1:T(4,128)(2,1)} copy(bf16[4,32,2,3,4096]{4,1,3,2,0:T(8,128)(2,1)} %bitcast.91) | data formatting | bytes 12582912 | tf_op jit(solution)/shard_map/reshape | solution.py:95
  103.6 9.0 %all-to-all-start.1 = ((bf16[4,32,2,3,4096]{4,0,3,2,1:T(4,128)(2,1)}), bf16[4,32,2,3,4096]{4,0,3,2,1:T(4,128)(2,1)}, u32[]{:S(2)}, u32[]{:S(2)}) async-start(bf16[4,32,2,3,4096]{4,0,3,2,1:T(4,128)(2,1)} %copy.15), calls=%async_computation.1 | async-start | bytes 12582912 | tf_op jit(solution)/shard_map/all_to_all | solution.py:96
  112.6 0.2 reduce-scatter.3.cloned.1.call-start
  113.5 77.0 %all-to-all-done.1 = bf16[4,32,2,3,4096]{4,0,3,2,1:T(4,128)(2,1)} async-done(((bf16[4,32,2,3,4096]{4,0,3,2,1:T(4,128)(2,1)}), bf16[4,32,2,3,4096]{4,0,3,2,1:T(4,128)(2,1)}, u32[]{:S(2)}, u32[]{:S(2)}) %all-to-all-start.1) | async-done | bytes 6291488 | tf_op jit(solution)/shard_map/all_to_all | solution.py:96
  190.5 6.9 %fusion.296 = (bf16[4,32,1,3,4096]{4,0,3,2,1:T(4,128)(2,1)}, bf16[4,32,1,3,4096]{4,0,3,2,1:T(4,128)(2,1)S(1)}) fusion(bf16[4,32,2,3,4096]{4,0,3,2,1:T(4,128)(2,1)} %all-to-all-done.1), kind=kLoop, calls=%fused_computation.284 | loop fusion | bytes 12582912 | tf_op jit(solution)/shard_map/slice | solution.py:34
  197.4 4.6 copy.17
  202.1 7.4 %reshape_squeeze.9 = bf16[384,4096]{1,0:T(8,128)(2,1)} reshape(bf16[4,32,1,3,4096]{4,3,1,0,2:T(4,128)(2,1)} %copy.17) | data formatting | bytes 6291456 | tf_op jit(solution)/shard_map/reshape;squeeze | solution.py:34
  209.5 7.5 %fusion.118 = f32[384,384]{1,0:T(8,128)S(1)} fusion(bf16[384,4096]{1,0:T(8,128)(2,1)} %reshape_squeeze.9, s32[4096]{0:T(1024)S(1)} %add_multiply_fusion.2, s32[]{:T(128)S(6)} %xor.269, s32[384]{0:T(512)S(1)} %iota_add_fusion, bf16[2,4096,384]{2,1,0:T(8,128)(2,1)} %param.12), kind=kOutput, calls=%fused_computation.151 | convolution fusion | flops 1239416832 | bytes 6899204 | tf_op jit(solution)/shard_map/dot_general | solution.py:37
  217.0 15.8 %convolution_convert_fusion.2 = bf16[384,4096]{1,0:T(8,128)(2,1)} fusion(s32[384]{0:T(512)S(1)} %get-tuple-element.9, s32[]{:T(128)S(6)} %xor.269, bf16[2,384,4096]{2,1,0:T(8,128)(2,1)} %param.14, bf16[384,4096]{1,0:T(8,128)(2,1)} %reshape_squeeze.9, s32[4096]{0:T(1024)S(1)} %add_multiply_fusion.2, s32[384]{0:T(512)S(1)} %iota_add_fusion, ...), kind=kOutput, calls=%fused_computation.92 | convolution fusion | flops 2484436992 | bytes 13193216 | tf_op jit(solution)/shard_map/dot_general | solution.py:41
  232.7 7.1 %stack_reshape_stack.13 = bf16[4,32,1,3,1,4096]{5,3,1,0,4,2:T(4,128)(2,1)} reshape(bf16[384,4096]{1,0:T(8,128)(2,1)} %convolution_convert_fusion.2) | data formatting | bytes 6291456 | tf_op jit(solution)/shard_map/stack;reshape;stack | solution.py:47
  239.8 7.4 %copy.16 = bf16[4,32,1,3,4096]{4,3,1,0,2:T(4,128)(2,1)} copy(bf16[4,32,1,3,4096]{4,0,3,2,1:T(4,128)(2,1)} %get-tuple-element.5) | data formatting | bytes 6291456 | tf_op jit(solution)/shard_map/slice | solution.py:34
  247.2 7.4 %reshape_squeeze.8 = bf16[384,4096]{1,0:T(8,128)(2,1)} reshape(bf16[4,32,1,3,4096]{4,3,1,0,2:T(4,128)(2,1)} %copy.16) | data formatting | bytes 6291456 | tf_op jit(solution)/shard_map/reshape;squeeze | solution.py:34
  254.6 7.5 %fusion.110 = f32[384,384]{1,0:T(8,128)S(1)} fusion(bf16[384,4096]{1,0:T(8,128)(2,1)} %reshape_squeeze.8, s32[]{:T(128)S(6)} %xor.269, s32[384]{0:T(512)S(1)} %iota_add_fusion, s32[4096]{0:T(1024)S(1)} %add_multiply_fusion.3, bf16[2,4096,384]{2,1,0:T(8,128)(2,1)} %param.12), kind=kOutput, calls=%fused_computation.147 | convolution fusion | flops 1239416832 | bytes 6899204 | tf_op jit(solution)/shard_map/dot_general | solution.py:37
  262.1 15.5 %convolution_convert_fusion.3 = bf16[384,4096]{1,0:T(8,128)(2,1)} fusion(s32[]{:T(128)S(6)} %xor.269, s32[384]{0:T(512)S(1)} %get-tuple-element.10, bf16[2,384,4096]{2,1,0:T(8,128)(2,1)} %param.14, bf16[384,4096]{1,0:T(8,128)(2,1)} %reshape_squeeze.8, s32[384]{0:T(512)S(1)} %iota_add_fusion, s32[4096]{0:T(1024)S(1)} %add_multiply_fusion.3, ...), kind=kOutput, calls=%fused_computation.93 | convolution fusion | flops 2484436992 | bytes 13193216 | tf_op jit(solution)/shard_map/dot_general | solution.py:41
  277.6 7.1 %stack_reshape_stack.12 = bf16[4,32,1,3,1,4096]{5,3,1,0,4,2:T(4,128)(2,1)} reshape(bf16[384,4096]{1,0:T(8,128)(2,1)} %convolution_convert_fusion.3) | data formatting | bytes 6291456 | tf_op jit(solution)/shard_map/stack;reshape;stack | solution.py:47
  284.7 8.7 %pad_maximum_fusion = bf16[4,32,2,3,1,4096]{5,3,1,0,4,2:T(4,128)(2,1)} fusion(bf16[4,32,1,3,1,4096]{5,3,1,0,4,2:T(4,128)(2,1)} %stack_reshape_stack.13, bf16[4,32,1,3,1,4096]{5,3,1,0,4,2:T(4,128)(2,1)} %stack_reshape_stack.12), kind=kLoop, calls=%fused_computation.20 | loop fusion | flops 3145728 | bytes 12582912 | tf_op jit(solution)/shard_map/stack | solution.py:47
  293.4 21.7 %copy.18 = bf16[4,32,2,3,1,4096]{5,0,4,3,2,1:T(4,128)(2,1)} copy(bf16[4,32,2,3,1,4096]{5,3,1,0,4,2:T(4,128)(2,1)} %pad_maximum_fusion) | data formatting | bytes 12582912 | tf_op jit(solution)/shard_map/stack | solution.py:47
  315.1 87.6 %all_to_all.21 = bf16[4,32,2,3,1,4096]{5,0,4,3,2,1:T(4,128)(2,1)S(1)} all-to-all(bf16[4,32,2,3,1,4096]{5,0,4,3,2,1:T(4,128)(2,1)} %copy.18), channel_id=1, replica_groups=mesh['dp'=4,'mp'=32] {'mp'}, dimensions={1} | all-to-all | bytes 12582912 | tf_op jit(solution)/shard_map/all_to_all | solution.py:100
  402.7 6.1 copy.19
  408.9 7.5 %fusion.120 = f32[384,384]{1,0:T(8,128)S(1)} fusion(bf16[384,4096]{1,0:T(8,128)(2,1)} %reshape_squeeze.9, s32[4096]{0:T(1024)S(1)} %add_multiply_fusion.2, s32[]{:T(128)S(6)} %xor.269, s32[384]{0:T(512)S(1)} %iota_add_fusion, bf16[2,4096,384]{2,1,0:T(8,128)(2,1)} %param.12), kind=kOutput, calls=%fused_computation.152 | convolution fusion | flops 1239416832 | bytes 6899204 | tf_op jit(solution)/shard_map/dot_general | solution.py:37
  416.4 15.5 %convolution_convert_fusion = bf16[384,4096]{1,0:T(8,128)(2,1)} fusion(s32[384]{0:T(512)S(1)} %get-tuple-element.9, s32[]{:T(128)S(6)} %xor.269, bf16[2,384,4096]{2,1,0:T(8,128)(2,1)} %param.14, bf16[384,4096]{1,0:T(8,128)(2,1)} %reshape_squeeze.9, s32[4096]{0:T(1024)S(1)} %add_multiply_fusion.2, s32[384]{0:T(512)S(1)} %iota_add_fusion, ...), kind=kOutput, calls=%fused_computation.90 | convolution fusion | flops 2484436992 | bytes 13193216 | tf_op jit(solution)/shard_map/dot_general | solution.py:41
  431.9 7.1 %stack_reshape_stack.15 = bf16[4,32,1,3,1,4096]{5,3,1,0,4,2:T(4,128)(2,1)} reshape(bf16[384,4096]{1,0:T(8,128)(2,1)} %convolution_convert_fusion) | data formatting | bytes 6291456 | tf_op jit(solution)/shard_map/stack;reshape;stack | solution.py:47
  439.0 7.5 %fusion.112 = f32[384,384]{1,0:T(8,128)S(1)} fusion(bf16[384,4096]{1,0:T(8,128)(2,1)} %reshape_squeeze.8, s32[]{:T(128)S(6)} %xor.269, s32[384]{0:T(512)S(1)} %iota_add_fusion, s32[4096]{0:T(1024)S(1)} %add_multiply_fusion.3, bf16[2,4096,384]{2,1,0:T(8,128)(2,1)} %param.12), kind=kOutput, calls=%fused_computation.148 | convolution fusion | flops 1239416832 | bytes 6899204 | tf_op jit(solution)/shard_map/dot_general | solution.py:37
  446.6 15.9 %convolution_convert_fusion.1 = bf16[384,4096]{1,0:T(8,128)(2,1)} fusion(s32[]{:T(128)S(6)} %xor.269, s32[384]{0:T(512)S(1)} %get-tuple-element.10, bf16[2,384,4096]{2,1,0:T(8,128)(2,1)} %param.14, bf16[384,4096]{1,0:T(8,128)(2,1)} %reshape_squeeze.8, s32[384]{0:T(512)S(1)} %iota_add_fusion, s32[4096]{0:T(1024)S(1)} %add_multiply_fusion.3, ...), kind=kOutput, calls=%fused_computation.91 | convolution fusion | flops 2484436992 | bytes 13193216 | tf_op jit(solution)/shard_map/dot_general | solution.py:41
  462.4 7.1 %stack_reshape_stack.14 = bf16[4,32,1,3,1,4096]{5,3,1,0,4,2:T(4,128)(2,1)} reshape(bf16[384,4096]{1,0:T(8,128)(2,1)} %convolution_convert_fusion.1) | data formatting | bytes 6291456 | tf_op jit(solution)/shard_map/stack;reshape;stack | solution.py:47
  469.5 8.7 %pad_maximum_fusion.1 = bf16[4,32,2,3,1,4096]{5,3,1,0,4,2:T(4,128)(2,1)} fusion(bf16[4,32,1,3,1,4096]{5,3,1,0,4,2:T(4,128)(2,1)} %stack_reshape_stack.15, bf16[4,32,1,3,1,4096]{5,3,1,0,4,2:T(4,128)(2,1)} %stack_reshape_stack.14), kind=kLoop, calls=%fused_computation.21 | loop fusion | flops 3145728 | bytes 12582912 | tf_op jit(solution)/shard_map/stack | solution.py:47
  478.2 21.3 %copy.21 = bf16[4,32,2,3,1,4096]{5,0,4,3,2,1:T(4,128)(2,1)} copy(bf16[4,32,2,3,1,4096]{5,3,1,0,4,2:T(4,128)(2,1)} %pad_maximum_fusion.1) | data formatting | bytes 12582912 | tf_op jit(solution)/shard_map/stack | solution.py:47
  499.5 77.7 %all_to_all.22 = bf16[4,32,2,3,1,4096]{5,0,4,3,2,1:T(4,128)(2,1)S(1)} all-to-all(bf16[4,32,2,3,1,4096]{5,0,4,3,2,1:T(4,128)(2,1)} %copy.21), channel_id=1, replica_groups=mesh['dp'=4,'mp'=32] {'mp'}, dimensions={1} | all-to-all | bytes 12582912 | tf_op jit(solution)/shard_map/all_to_all | solution.py:100
  577.3 6.1 copy.22
  583.4 0.6 copy-done.5
  584.1 4.1 copy.20
  588.2 3.3 convert_element_type.262
  591.6 52.5 %reduce-scatter.5.cloned.1.call-done = bf16[1,32,2,3,1,4096]{5,1,4,3,2,0:T(8,128)(2,1)} async-done(((bf16[4,32,2,3,1,4096]{5,1,4,3,2,0:T(8,128)(2,1)}), bf16[1,32,2,3,1,4096]{5,1,4,3,2,0:T(8,128)(2,1)}) %reduce-scatter.5.cloned.1.call-update) | async-done | bytes 1572880 | tf_op jit(solution)/shard_map/reduce_scatter | solution.py:101
  644.0 4.1 copy.23
  648.1 4.3 convert_element_type.279
  652.4 2.2 gather_fusion
  654.6 3.9 gather_fusion.1
  658.5 1.9 multiply_convert_fusion
  (22 shorter events, 0.2 us)
Async XLA Ops:
  7.2 3.6 copy-start
  10.2 0.6 copy-start.4
  103.6 87.0 %all-to-all-start.1 = ((bf16[4,32,2,3,4096]{4,0,3,2,1:T(4,128)(2,1)}), bf16[4,32,2,3,4096]{4,0,3,2,1:T(4,128)(2,1)}, u32[]{:S(2)}, u32[]{:S(2)}) async-start(bf16[4,32,2,3,4096]{4,0,3,2,1:T(4,128)(2,1)} %copy.15), calls=%async_computation.1 | async-start | bytes 12582912 | tf_op jit(solution)/shard_map/all_to_all | solution.py:96
  112.6 471.5 %reduce-scatter.3.cloned.1.call-start = ((), (), s32[]{:S(2)}) async-start(), calls=%async_computation.6 | async-start | bytes 7864320 | tf_op jit(solution)/shard_map/reduce_scatter | solution.py:101
  408.9 235.2 %reduce-scatter.5.cloned.1.call-start = ((), (), s32[]{:S(2)}) async-start(), calls=%async_computation.7 | async-start | bytes 7864320 | tf_op jit(solution)/shard_map/reduce_scatter | solution.py:101
  583.4 0.7 copy-start.5
  652.4 8.0 %copy-start.1 = (bf16[128,4096]{1,0:T(8,128)(2,1)S(1)}, bf16[128,4096]{1,0:T(8,128)(2,1)}, u32[]{:S(2)}) copy-start(bf16[128,4096]{1,0:T(8,128)(2,1)} %param.9) | copy-start | bytes 3145732
  654.6 3.9 copy-start.2
  654.6 3.9 copy-start.3
  654.6 3.9 copy-start.6
Sparse Core Ops, SparseCore 0:
  409.0 59.9 reduce-scatter.2
  583.5 60.4 reduce-scatter.4
